TPU v7x, 256 devices: a whole 4x4x8 slice. The times are simulated.
256 devices in a mesh: seq: 16 (over z, core), head: 4 (over x), dp: 4 (over y).
Axes of the slice: x: 4, y: 4, z: 8, core: 2. Of those that a mesh axis runs over, the one named last changes fastest.
Arguments:
- self_queries: bfloat16 [4, 2048, 2560], P('dp', ('seq', 'head')), may hold values from -8 to 8
- self_keys: bfloat16 [4, 2048, 2560], P('dp', ('seq', 'head')), may hold values from -4 to 4
- self_values: bfloat16 [4, 2048, 2560], P('dp', ('seq', 'head')), may hold values from -6 to 6
- self_cotangent: bfloat16 [4, 2048, 2560], P('dp', ('seq', 'head')), may hold values from -6 to 6
- text_queries: bfloat16 [4, 4096, 2560], P('dp', 'seq', 'head'), may hold values from -8 to 8
- memory_keys: bfloat16 [4, 2048, 2560], P('dp', 'seq', 'head'), may hold values from -4 to 4
- memory_values: bfloat16 [4, 2048, 2560], P('dp', 'seq', 'head'), may hold values from -6 to 6
- text_cotangent: bfloat16 [4, 4096, 2560], P('dp', 'seq', 'head'), may hold values from -6 to 6
- slopes: float32 [2, 20], P(None, 'head'), may hold values from 0.01 to 0.3
- page_counts: int32 [4, 4], P('dp'), may hold values from 1 to 1024, as said below
- page_cols: int32 [4, 4], P('dp'), may hold values from 4 to 64
- text_page: int32 [4, 4096], P('dp'), may hold values from 0 to 3, as said below
Outputs:
- self_query_grad: bfloat16 [4, 2048, 2560], P('dp', ('seq', 'head'))
- self_key_grad: bfloat16 [4, 2048, 2560], P('dp', ('seq', 'head'))
- self_value_grad: bfloat16 [4, 2048, 2560], P('dp', ('seq', 'head'))
- slope_grad: float32 [2, 20], P(None, 'head')
- text_query_grad: bfloat16 [4, 4096, 2560], P('dp', 'seq', 'head')
- memory_key_grad: bfloat16 [4, 2048, 2560], P('dp', 'seq', 'head')
- memory_value_grad: bfloat16 [4, 2048, 2560], P('dp', 'seq', 'head')
Inputs may be any that keep to these rules, and one draw needn't show every extreme that they name: `page_counts`: each pack's counts sum to 2048; one page of every pack has exactly 1024 patches. `text_page`: never falls along a pack's text rows; every page has at least one text row.
All inputs are finite; a program needn't handle non-finite values.
Results may differ from a plain program's by a relative error of at most 0.006.
Values may be sent and summed in bfloat16 or wider, within the bound.
No kernel may reach another device: no remote copies, remote signals or barrier semaphores. Data moves between devices by JAX's collectives and lax.ppermute only.
A program may use at most 128 MiB of HBM per device.

v0:
```python
import jax
import jax.numpy as jnp
from jax import lax
from jax.sharding import PartitionSpec as P

MASK_FILL = -1e30


def page_layout(counts, widths, patch_total):
    page_ends = jnp.cumsum(counts)
    starts = page_ends - counts
    positions = jnp.arange(patch_total, dtype=jnp.int32)
    page_ids = jnp.sum((positions[:, None] >= page_ends[None, :]).astype(jnp.int32), axis=1)
    one_hot = page_ids[:, None] == jnp.arange(counts.shape[0], dtype=jnp.int32)[None, :]
    page_start = jnp.sum(jnp.where(one_hot, starts[None, :], 0), axis=1)
    page_width = jnp.sum(jnp.where(one_hot, widths[None, :], 0), axis=1)
    offsets = positions - page_start
    return (page_ids, offsets // page_width, offsets % page_width)


def take_rows(vector, row_start, row_count):
    return lax.dynamic_slice_in_dim(vector, row_start, row_count, 0)


def heads_of(matrix, head_count):
    return matrix.reshape(matrix.shape[0], head_count, -1)


def alibi(slopes, query_layout, key_layout):
    row_gap = jnp.abs(query_layout[1][:, None] - key_layout[1][None, :]).astype(jnp.float32)
    col_gap = jnp.abs(query_layout[2][:, None] - key_layout[2][None, :]).astype(jnp.float32)
    same_page = query_layout[0][:, None] == key_layout[0][None, :]
    decay = -(slopes[0][:, None, None] * row_gap[None] + slopes[1][:, None, None] * col_gap[None])
    return (jnp.where(same_page[None], decay, MASK_FILL), row_gap, col_gap)


def query_side(queries, key_rows, value_rows, grad_rows, logit_bias):
    inv_root = queries.shape[2] ** (-0.5)
    scores = (
        jnp.einsum("rhs,khs->hrk", queries, key_rows, preferred_element_type=jnp.float32) * inv_root
        + logit_bias
    )
    row_max = jnp.max(scores, axis=2, keepdims=True)
    weights = jnp.exp(scores - row_max)
    row_total = jnp.sum(weights, axis=2, keepdims=True)
    softmax_w = weights / row_total
    log_total = (row_max + jnp.log(row_total))[:, :, 0]
    grad_probs = jnp.einsum(
        "rhs,khs->hrk", grad_rows, value_rows, preferred_element_type=jnp.float32
    )
    row_delta = jnp.sum(softmax_w * grad_probs, axis=2, keepdims=True)
    grad_scores = softmax_w * (grad_probs - row_delta)
    grad_scores_b = grad_scores.astype(jnp.bfloat16)
    query_grad = (
        jnp.einsum("hrk,khs->rhs", grad_scores_b, key_rows, preferred_element_type=jnp.float32)
        * inv_root
    )
    return (
        query_grad,
        grad_scores,
        grad_scores_b,
        softmax_w.astype(jnp.bfloat16),
        log_total,
        row_delta[:, :, 0],
    )


def key_terms(grad_scores_b, softmax_b, queries, grad_rows, row_count):
    inv_root = queries.shape[3] ** (-0.5)
    key_grad = (
        jnp.einsum("chrk,crhs->khs", grad_scores_b, queries, preferred_element_type=jnp.float32)
        * inv_root
    )
    value_grad = jnp.einsum(
        "chrk,crhs->khs", softmax_b, grad_rows, preferred_element_type=jnp.float32
    )
    return jnp.stack([key_grad.reshape(row_count, -1), value_grad.reshape(row_count, -1)], axis=1)


def local(
    self_queries,
    self_keys,
    self_values,
    self_cotangent,
    text_queries,
    memory_keys,
    memory_values,
    text_cotangent,
    slopes,
    page_counts,
    page_cols,
    text_page,
):
    head_count = slopes.shape[1]
    regrouped = (
        lax.all_to_all(self_queries[0], "head", split_axis=1, concat_axis=0, tiled=True),
        lax.all_to_all(self_keys[0], "head", split_axis=1, concat_axis=0, tiled=True),
        lax.all_to_all(self_values[0], "head", split_axis=1, concat_axis=0, tiled=True),
        lax.all_to_all(self_cotangent[0], "head", split_axis=1, concat_axis=0, tiled=True),
    )
    local_queries, local_keys, local_values, local_grads = regrouped
    patch_rows = local_queries.shape[0]
    all_keys, all_values = (
        lax.all_gather(local_keys, "seq", axis=0, tiled=True),
        lax.all_gather(local_values, "seq", axis=0, tiled=True),
    )
    patch_total = all_keys.shape[0]
    whole_layout = page_layout(page_counts[0], page_cols[0], patch_total)
    own_start = lax.axis_index("seq") * patch_rows
    own_layout = tuple((take_rows(item, own_start, patch_rows) for item in whole_layout))
    self_bias, row_gap, col_gap = alibi(slopes, own_layout, whole_layout)
    query_heads = heads_of(local_queries, head_count)
    grad_heads = heads_of(local_grads, head_count)
    self_dq, self_ds, self_ds_b, self_p_b, self_lse, self_delta = query_side(
        query_heads,
        heads_of(all_keys, head_count),
        heads_of(all_values, head_count),
        grad_heads,
        self_bias,
    )
    slope_local = -jnp.stack(
        [
            jnp.sum(self_ds * row_gap[None], axis=(1, 2)),
            jnp.sum(self_ds * col_gap[None], axis=(1, 2)),
        ]
    )
    self_ds_blocks = self_ds_b[None]
    self_p_blocks = self_p_b[None]
    query_blocks = query_heads[None]
    grad_blocks = grad_heads[None]
    self_pair = lax.psum_scatter(
        key_terms(
            self_ds_blocks,
            self_p_blocks,
            query_blocks,
            grad_blocks,
            patch_rows * lax.axis_size("seq"),
        ),
        "seq",
        scatter_dimension=0,
        tiled=True,
    )
    self_dk = self_pair[:, 0]
    self_dv = self_pair[:, 1]
    restored = (
        lax.all_to_all(
            self_dq.reshape(patch_rows, -1).astype(jnp.bfloat16),
            "head",
            split_axis=0,
            concat_axis=1,
            tiled=True,
        ),
        lax.all_to_all(
            self_dk.astype(jnp.bfloat16), "head", split_axis=0, concat_axis=1, tiled=True
        ),
        lax.all_to_all(
            self_dv.astype(jnp.bfloat16), "head", split_axis=0, concat_axis=1, tiled=True
        ),
    )
    slope_grad = lax.psum(slope_local, ("seq", "dp")) / patch_total
    memory_all_keys, memory_all_values = (
        lax.all_gather(memory_keys[0], "seq", axis=0, tiled=True),
        lax.all_gather(memory_values[0], "seq", axis=0, tiled=True),
    )
    memory_all_key_heads = heads_of(memory_all_keys, head_count)
    memory_all_value_heads = heads_of(memory_all_values, head_count)
    text_rows = text_queries.shape[1]
    text_start = lax.axis_index("seq") * text_rows
    text_ids = text_page[0]
    own_text = take_rows(text_ids, text_start, text_rows)
    text_query_heads = heads_of(text_queries[0], head_count)
    text_grad_heads = heads_of(text_cotangent[0], head_count)
    block_count = text_rows // text_rows
    text_query_blocks = text_query_heads.reshape(block_count, text_rows, head_count, -1)
    text_grad_blocks = text_grad_heads.reshape(block_count, text_rows, head_count, -1)

    def cross_block(inputs):
        block_queries, block_grads, block_pages = inputs
        block_bias = jnp.where(
            block_pages[:, None] == whole_layout[0][None, :], 0.0, MASK_FILL
        ).astype(jnp.float32)[None]
        result = query_side(
            block_queries, memory_all_key_heads, memory_all_value_heads, block_grads, block_bias
        )
        return (result[0], result[2], result[3], result[4], result[5])

    cross_out = lax.map(
        cross_block, (text_query_blocks, text_grad_blocks, own_text.reshape(block_count, text_rows))
    )
    text_dq = cross_out[0].reshape(text_rows, -1)
    text_ds_b = cross_out[1]
    text_p_b = cross_out[2]
    memory_pair = lax.psum_scatter(
        key_terms(
            text_ds_b,
            text_p_b,
            text_query_blocks,
            text_grad_blocks,
            patch_rows * lax.axis_size("seq"),
        ),
        "seq",
        scatter_dimension=0,
        tiled=True,
    )
    memory_dk = memory_pair[:, 0]
    memory_dv = memory_pair[:, 1]
    return (
        restored[0][None],
        restored[1][None],
        restored[2][None],
        slope_grad,
        text_dq.astype(jnp.bfloat16)[None],
        memory_dk.astype(jnp.bfloat16)[None],
        memory_dv.astype(jnp.bfloat16)[None],
    )


def solution(mesh):
    in_specs = (
        P("dp", ("seq", "head"), None),
        P("dp", ("seq", "head"), None),
        P("dp", ("seq", "head"), None),
        P("dp", ("seq", "head"), None),
        P("dp", "seq", "head"),
        P("dp", "seq", "head"),
        P("dp", "seq", "head"),
        P("dp", "seq", "head"),
        P(None, "head"),
        P("dp", None),
        P("dp", None),
        P("dp", None),
    )
    out_specs = (
        P("dp", ("seq", "head"), None),
        P("dp", ("seq", "head"), None),
        P("dp", ("seq", "head"), None),
        P(None, "head"),
        P("dp", "seq", "head"),
        P("dp", "seq", "head"),
        P("dp", "seq", "head"),
    )
    return jax.shard_map(local, mesh=mesh, in_specs=in_specs, out_specs=out_specs, check_vma=False)
```

profile of v0, /device:TPU:2, one launch (start us, length us, event | category | flops | bytes accessed | tf_op | source)
XLA Modules:
  0.0 406.0 jit_solution(9305916653580052399)
XLA Ops:
  7.3 1.0 all_to_all.85
  8.3 10.0 %all_to_all.109 = bf16[32,4,640]{2,0,1:T(8,128)(2,1)} all-to-all(bf16[32,4,640]{2,0,1:T(8,128)(2,1)S(1)} %copy.117), channel_id=1, replica_groups=mesh['seq'=16,'head'=4,'dp'=4] {'head'}, dimensions={1} | all-to-all | bytes 327680 | tf_op jit(solution)/shard_map/all_to_all | solution.py:97
  18.4 1.0 all_to_all.92
  19.4 9.2 %all_to_all.110 = bf16[32,4,640]{2,0,1:T(8,128)(2,1)} all-to-all(bf16[32,4,640]{2,0,1:T(8,128)(2,1)S(1)} %copy.122), channel_id=1, replica_groups=mesh['seq'=16,'head'=4,'dp'=4] {'head'}, dimensions={1} | all-to-all | bytes 327680 | tf_op jit(solution)/shard_map/all_to_all | solution.py:98
  28.6 1.7 copy.136
  30.4 1.0 all_to_all.82
  31.4 0.7 copy.116
  32.1 4.7 %all-to-all-start = ((bf16[32,4,640]{2,0,1:T(8,128)(2,1)}), bf16[32,4,640]{2,0,1:T(8,128)(2,1)S(1)}, u32[]{:S(2)}, u32[]{:S(2)}) async-start(bf16[32,4,640]{2,0,1:T(8,128)(2,1)} %copy.116), calls=%async_computation | async-start | bytes 327680 | tf_op jit(solution)/shard_map/all_to_all | solution.py:96
  36.8 1.7 copy.140
  38.6 0.8 reduce-window.4
  39.4 0.7 fusion.25
  40.2 0.8 select_reduce_fusion.1
  41.4 1.8 abs_convert_fusion
  43.5 0.7 copy.121
  44.2 4.8 %all-to-all-start.2 = ((bf16[32,4,640]{2,0,1:T(8,128)(2,1)}), bf16[32,4,640]{2,0,1:T(8,128)(2,1)S(1)}, u32[]{:S(2)}, u32[]{:S(2)}) async-start(bf16[32,4,640]{2,0,1:T(8,128)(2,1)} %copy.121), calls=%async_computation.2 | async-start | bytes 327680 | tf_op jit(solution)/shard_map/all_to_all | solution.py:99
  49.4 4.3 %all-to-all-done.2 = bf16[32,4,640]{2,0,1:T(8,128)(2,1)S(1)} async-done(((bf16[32,4,640]{2,0,1:T(8,128)(2,1)}), bf16[32,4,640]{2,0,1:T(8,128)(2,1)S(1)}, u32[]{:S(2)}, u32[]{:S(2)}) %all-to-all-start.2) | async-done | bytes 163872 | tf_op jit(solution)/shard_map/all_to_all | solution.py:99
  54.1 6.2 %all-gather.7.cloned.1.call-done = bf16[2048,640]{1,0:T(8,128)(2,1)} async-done(((bf16[128,640]{1,0:T(8,128)(2,1)}), bf16[2048,640]{1,0:T(8,128)(2,1)}) %all-gather.7.cloned.1.call-update) | async-done | bytes 2621456 | tf_op jit(solution)/shard_map/all_gather | solution.py:104
  60.3 3.0 copy.118
  63.3 37.8 %all-gather.9.cloned.1.call-done = bf16[2048,640]{1,0:T(8,128)(2,1)} async-done(((bf16[128,640]{1,0:T(8,128)(2,1)}), bf16[2048,640]{1,0:T(8,128)(2,1)}) %all-gather.9.cloned.1.call-update) | async-done | bytes 2621456 | tf_op jit(solution)/shard_map/all_gather | solution.py:105
  101.0 4.5 %copy.123 = bf16[2048,640]{0,1:T(8,128)(2,1)} copy(bf16[2048,640]{1,0:T(8,128)(2,1)} %all-gather.9.cloned.1.call-done) | data formatting | bytes 5242880 | tf_op jit(solution)/shard_map/all_gather | solution.py:105
  105.5 3.6 select_add_fusion
  109.1 1.6 fusion.28
  110.7 1.0 copy-done.4
  111.7 1.0 copy-done.7
  112.7 1.3 multiply_reduce_fusion.3
  114.3 2.4 multiply_reduce_fusion.2
  116.7 3.2 convolution_multiply_fusion
  119.8 6.0 %copy.131 = f32[2048,1,640]{2,0,1:T(8,128)} copy(f32[2048,1,640]{0,2,1:T(8,128)} %bitcast.79) | data formatting | bytes 10485760 | tf_op jit(solution)/shard_map/stack;reshape | solution.py:77
  125.8 8.0 %fusion.7 = f32[5,2048,128]{1,2,0:T(8,128)} fusion(bf16[128,5,128]{0,2,1:T(8,128)(2,1)S(1)} %copy.130, f32[5,128]{1,0:T(8,128)S(1)} %get-tuple-element.85, f32[5,128,2048]{2,1,0:T(8,128)} %copy-done.4), kind=kOutput, calls=%fused_computation.22 | convolution fusion | flops 339479168 | bytes 10652160 | tf_op jit(solution)/shard_map/chrk,crhs->khs/dot_general | solution.py:74
  133.7 5.9 %copy.132 = f32[2048,1,640]{2,0,1:T(8,128)} copy(f32[2048,1,640]{0,2,1:T(8,128)} %bitcast.84) | data formatting | bytes 10485760 | tf_op jit(solution)/shard_map/stack;reshape | solution.py:77
  139.6 8.8 %pad_maximum_fusion = f32[2048,2,640]{2,0,1:T(8,128)} fusion(f32[2048,1,640]{2,0,1:T(8,128)} %copy.132, f32[2048,1,640]{2,0,1:T(8,128)} %copy.131), kind=kLoop, calls=%fused_computation.2 | loop fusion | flops 2621440 | bytes 20971520 | tf_op jit(solution)/shard_map/stack | solution.py:77
  148.7 0.7 copy-done.8
  149.6 1.1 copy.139
  150.8 1.6 compare_select_fusion
  152.4 9.5 %fusion.29 = (f32[5,256]{1,0:T(8,128)S(1)}, f32[5,256,2048]{2,1,0:T(8,128)}) fusion(f32[256,2048]{1,0:T(8,128)} %compare_select_fusion, bf16[256,5,128]{0,2,1:T(8,128)(2,1)S(1)} %bitcast.87, bf16[2048,5,128]{0,2,1:T(8,128)(2,1)} %bitcast.104), kind=kOutput, calls=%fused_computation.62 | convolution fusion | flops 681576448 | bytes 15537152 | tf_op jit(solution)/shard_map/while/body/eval_jaxpr/sub | solution.py:44
  161.8 27.1 %all-gather.13.cloned.1.call-done = bf16[1,2048,640]{1,2,0:T(8,128)(2,1)} async-done(((bf16[1,128,640]{1,2,0:T(8,128)(2,1)}), bf16[1,2048,640]{1,2,0:T(8,128)(2,1)}) %all-gather.13.cloned.1.call-update) | async-done | bytes 2621456 | tf_op jit(solution)/shard_map/all_gather | solution.py:163
  189.0 6.1 %multiply_reduce_fusion = (f32[5,256]{1,0:T(8,128)S(1)}, f32[5,256,2048]{2,1,0:T(8,128)S(1)}) fusion(f32[5,256,2048]{2,1,0:T(8,128)} %get-tuple-element.90, f32[5,256]{1,0:T(8,128)S(1)} %get-tuple-element.89, bf16[256,5,128]{0,2,1:T(8,128)(2,1)S(1)} %bitcast.96, bf16[2048,5,128]{0,2,1:T(8,128)(2,1)} %bitcast.106), kind=kOutput, calls=%fused_computation.5 | convolution fusion | flops 678951680 | bytes 23930880 | tf_op jit(solution)/shard_map/while/body/eval_jaxpr/rhs,khs->hrk/dot_general | solution.py:48
  195.1 1.1 slice-done.1
  196.2 0.6 slice-done.2
  196.8 1.8 multiply_convert_fusion
  198.6 3.9 convolution_multiply_fusion.1
  202.6 5.9 %copy.143 = f32[2048,1,640]{2,0,1:T(8,128)} copy(f32[2048,1,640]{0,2,1:T(8,128)} %bitcast.78) | data formatting | bytes 10485760 | tf_op jit(solution)/shard_map/stack;reshape | solution.py:77
  208.5 7.4 %fusion.3 = f32[5,2048,128]{1,2,0:T(8,128)} fusion(bf16[256,5,128]{0,2,1:T(8,128)(2,1)S(1)} %bitcast.97, f32[5,256,2048]{2,1,0:T(8,128)} %get-tuple-element.90, f32[5,256]{1,0:T(8,128)S(1)} %get-tuple-element.89), kind=kOutput, calls=%fused_computation.9 | convolution fusion | flops 676331520 | bytes 16061440 | tf_op jit(solution)/shard_map/chrk,crhs->khs/dot_general | solution.py:74
  215.9 5.9 %copy.144 = f32[2048,1,640]{2,0,1:T(8,128)} copy(f32[2048,1,640]{0,2,1:T(8,128)} %bitcast.85) | data formatting | bytes 10485760 | tf_op jit(solution)/shard_map/stack;reshape | solution.py:77
  221.9 8.7 %pad_maximum_fusion.1 = f32[2048,2,640]{2,0,1:T(8,128)} fusion(f32[2048,1,640]{2,0,1:T(8,128)} %copy.144, f32[2048,1,640]{2,0,1:T(8,128)} %copy.143), kind=kLoop, calls=%fused_computation.3 | loop fusion | flops 2621440 | bytes 20971520 | tf_op jit(solution)/shard_map/stack | solution.py:77
  230.6 5.3 %fusion.14 = bf16[5,256,128]{1,2,0:T(8,128)(2,1)S(1)} fusion(bf16[5,256,2048]{2,1,0:T(8,128)(2,1)} %copy-done.2, bf16[2048,5,128]{0,2,1:T(8,128)(2,1)} %bitcast.105), kind=kOutput, calls=%fused_computation.31 | convolution fusion | flops 671416320 | bytes 8192000 | tf_op jit(solution)/shard_map/while/body/eval_jaxpr/hrk,khs->rhs/dot_general | solution.py:55
  236.0 0.9 copy.145
  236.9 129.5 %psum.7 = f32[2,5]{1,0:T(2,128)S(1)} all-reduce(f32[2,5]{1,0:T(2,128)S(1)} %maximum_negate_fusion), channel_id=1, replica_groups=mesh['seq'=16,'head'=4,'dp'=4] {'seq','dp'}, use_global_device_ids=true, to_apply=%region_10.11 | all-reduce | flops 10 | bytes 80 | tf_op jit(solution)/shard_map/psum | solution.py:160
  366.3 2.6 fusion.21
  369.0 0.9 convert_element_type.95
  369.9 4.8 %all-to-all-start.4 = ((bf16[4,32,640]{2,1,0:T(8,128)(2,1)}), bf16[4,32,640]{2,1,0:T(8,128)(2,1)S(1)}, u32[]{:S(2)}, u32[]{:S(2)}) async-start(bf16[4,32,640]{2,1,0:T(8,128)(2,1)} %convert_element_type.95), calls=%async_computation.4 | async-start | bytes 327680 | tf_op jit(solution)/shard_map/all_to_all | solution.py:146
  374.7 1.1 convert.8
  375.8 0.8 fusion.27
  376.6 2.8 all-to-all-done.4
  379.4 4.8 %all-to-all-start.5 = ((bf16[4,32,640]{2,1,0:T(8,128)(2,1)}), bf16[4,32,640]{2,1,0:T(8,128)(2,1)S(1)}, u32[]{:S(2)}, u32[]{:S(2)}) async-start(bf16[4,32,640]{2,1,0:T(8,128)(2,1)} %bitcast.21), calls=%async_computation.6 | async-start | bytes 327680 | tf_op jit(solution)/shard_map/all_to_all | solution.py:153
  384.2 0.6 broadcast_multiply_fusion
  384.8 0.7 broadcast_in_dim.107
  385.6 1.1 convert.9
  386.7 2.2 all-to-all-done.5
  388.9 4.8 %all-to-all-start.6 = ((bf16[4,32,640]{2,1,0:T(8,128)(2,1)}), bf16[4,32,640]{2,1,0:T(8,128)(2,1)S(1)}, u32[]{:S(2)}, u32[]{:S(2)}) async-start(bf16[4,32,640]{2,1,0:T(8,128)(2,1)} %bitcast.23), calls=%async_computation.7 | async-start | bytes 327680 | tf_op jit(solution)/shard_map/all_to_all | solution.py:156
  393.7 0.7 slice_bitcast_fusion
  394.5 0.7 broadcast_in_dim.108
  395.2 3.1 all-to-all-done.6
  398.4 0.7 broadcast_in_dim.109
  (61 shorter events, 3.1 us)
Async XLA Ops:
  7.2 143.6 %copy-start = (s32[1,4096]{1,0:T(1,128)S(1)}, s32[1,4096]{1,0:T(1,128)}, u32[]{:S(2)}) copy-start(s32[1,4096]{1,0:T(1,128)} %param.23) | copy-start | bytes 49156
  7.2 36.3 %copy-start.9 = (bf16[1,32,2560]{2,1,0:T(8,128)(2,1)S(1)}, bf16[1,32,2560]{2,1,0:T(8,128)(2,1)}, u32[]{:S(2)}) copy-start(bf16[1,32,2560]{2,1,0:T(8,128)(2,1)} %param.15) | copy-start | bytes 491524
  7.2 41.8 %copy-start.10 = (f32[2,5]{1,0:T(2,128)S(1)}, f32[2,5]{1,0:T(2,128)}, u32[]{:S(2)}) copy-start(f32[2,5]{1,0:T(2,128)} %param.20) | copy-start | bytes 124
  7.2 53.1 %all-gather.7.cloned.1.call-start = ((), (), s32[]{:S(2)}) async-start(), calls=%async_computation.9 | async-start | bytes 2785280 | tf_op jit(solution)/shard_map/all_gather | solution.py:104
  18.3 82.7 %all-gather.9.cloned.1.call-start = ((), (), s32[]{:S(2)}) async-start(), calls=%async_computation.10 | async-start | bytes 2785280 | tf_op jit(solution)/shard_map/all_gather | solution.py:105
  28.6 123.8 %all-gather.11.cloned.1.call-start = ((), (), s32[]{:S(2)}) async-start(), calls=%async_computation.13 | async-start | bytes 2785280 | tf_op jit(solution)/shard_map/all_gather | solution.py:162
  32.1 12.1 %all-to-all-start = ((bf16[32,4,640]{2,0,1:T(8,128)(2,1)}), bf16[32,4,640]{2,0,1:T(8,128)(2,1)S(1)}, u32[]{:S(2)}, u32[]{:S(2)}) async-start(bf16[32,4,640]{2,0,1:T(8,128)(2,1)} %copy.116), calls=%async_computation | async-start | bytes 327680 | tf_op jit(solution)/shard_map/all_to_all | solution.py:96
  36.8 152.2 %all-gather.13.cloned.1.call-start = ((), (), s32[]{:S(2)}) async-start(), calls=%async_computation.14 | async-start | bytes 2785280 | tf_op jit(solution)/shard_map/all_gather | solution.py:163
  44.2 9.5 %all-to-all-start.2 = ((bf16[32,4,640]{2,0,1:T(8,128)(2,1)}), bf16[32,4,640]{2,0,1:T(8,128)(2,1)S(1)}, u32[]{:S(2)}, u32[]{:S(2)}) async-start(bf16[32,4,640]{2,0,1:T(8,128)(2,1)} %copy.121), calls=%async_computation.2 | async-start | bytes 327680 | tf_op jit(solution)/shard_map/all_to_all | solution.py:99
  49.0 325.7 %reduce-scatter.3.cloned.1.call-start = ((), (), s32[]{:S(2)}) async-start(), calls=%async_computation.11 | async-start | bytes 11141120 | tf_op jit(solution)/shard_map/reduce_scatter | solution.py:131
  63.3 45.8 %copy-start.3 = (bf16[2048,640]{0,1:T(8,128)(2,1)}, bf16[2048,640]{0,1:T(8,128)(2,1)S(1)}, u32[]{:S(2)}) copy-start(bf16[2048,640]{0,1:T(8,128)(2,1)S(1)} %copy.118) | copy-start | bytes 7864324
  109.1 2.7 copy-start.4
  109.1 3.6 copy-start.7
  112.7 1.3 copy-start.5
  112.7 1.6 copy-start.6
  148.4 1.0 copy-start.8
  148.5 237.1 %reduce-scatter.5.cloned.1.call-start = ((), (), s32[]{:S(2)}) async-start(), calls=%async_computation.12 | async-start | bytes 11141120 | tf_op jit(solution)/shard_map/reduce_scatter | solution.py:193
  189.0 6.1 %slice-start = ((s8[10485760]{0:T(1024)(128)(4,1)}), s8[4194304]{0:T(1024)(128)(4,1)S(1)}, s32[]{:S(2)}) async-start(s8[10485760]{0:T(1024)(128)(4,1)} %bitcast.80), calls=%async_computation.15 | async-start | bytes 8388608
  189.0 7.3 %slice-start.1 = ((s8[10485760]{0:T(1024)(128)(4,1)}), s8[4194304]{0:T(1024)(128)(4,1)S(1)}, s32[]{:S(2)}) async-start(s8[10485760]{0:T(1024)(128)(4,1)} %bitcast.80), calls=%async_computation.16 | async-start | bytes 8388608
  189.0 7.9 %slice-start.2 = ((s8[10485760]{0:T(1024)(128)(4,1)}), s8[2097152]{0:T(1024)(128)(4,1)S(1)}, s32[]{:S(2)}) async-start(s8[10485760]{0:T(1024)(128)(4,1)} %bitcast.80), calls=%async_computation.17 | async-start | bytes 4194304
  198.6 4.0 copy-start.2
  236.9 162.3 %copy-start.1 = (s32[1,4096]{1,0:T(1,128)S(1)}, s32[1,4096]{1,0:T(1,128)}, u32[]{:S(2)}) copy-start(s32[1,4096]{1,0:T(1,128)} %param.23) | copy-start | bytes 49156
  369.9 9.5 %all-to-all-start.4 = ((bf16[4,32,640]{2,1,0:T(8,128)(2,1)}), bf16[4,32,640]{2,1,0:T(8,128)(2,1)S(1)}, u32[]{:S(2)}, u32[]{:S(2)}) async-start(bf16[4,32,640]{2,1,0:T(8,128)(2,1)} %convert_element_type.95), calls=%async_computation.4 | async-start | bytes 327680 | tf_op jit(solution)/shard_map/all_to_all | solution.py:146
  379.4 9.5 %all-to-all-start.5 = ((bf16[4,32,640]{2,1,0:T(8,128)(2,1)}), bf16[4,32,640]{2,1,0:T(8,128)(2,1)S(1)}, u32[]{:S(2)}, u32[]{:S(2)}) async-start(bf16[4,32,640]{2,1,0:T(8,128)(2,1)} %bitcast.21), calls=%async_computation.6 | async-start | bytes 327680 | tf_op jit(solution)/shard_map/all_to_all | solution.py:153
  388.9 9.5 %all-to-all-start.6 = ((bf16[4,32,640]{2,1,0:T(8,128)(2,1)}), bf16[4,32,640]{2,1,0:T(8,128)(2,1)S(1)}, u32[]{:S(2)}, u32[]{:S(2)}) async-start(bf16[4,32,640]{2,1,0:T(8,128)(2,1)} %bitcast.23), calls=%async_computation.7 | async-start | bytes 327680 | tf_op jit(solution)/shard_map/all_to_all | solution.py:156
Sparse Core Ops, SparseCore 0:
  18.5 41.7 all-gather.6
  62.1 38.8 all-gather.8
  103.4 41.4 all-gather.10
  147.0 41.9 all-gather.12
  191.4 73.8 reduce-scatter.2
  267.7 74.0 reduce-scatter.4
where the time goes:
time: 408 us; the launch traced here: 406 us
  blocking collectives  149 us (37%)
  waiting for transfers between devices  83.5 us (20%)
  local copies, waits for them, and re-layouts  52.1 us (13%)
  matrix products  50.7 us (12%)
  other arithmetic  32.3 us (8%)
  starting transfers between devices  24.2 us (6%)
  between operations  14.4 us (4%)
    psum x1, blocking collectives, local(): slope_grad = lax.psum(slope_local, ('seq', 'dp')) / patch_total  129 us
    all_gather x1, waiting for transfers between devices, local(): lax.all_gather(local_values, 'seq', axis=0, tiled=True)  37.8 us
    all_gather x1, waiting for transfers between devices, local(): lax.all_gather(memory_values[0], 'seq', axis=0, tiled=True)  27.1 us
    another operation x4, local copies, waits for them, and re-layouts, key_terms(): jnp.stack([key_grad.reshape(row_count, -1), value_grad.reshape(row_count,...  23.7 us
    another operation x2, other arithmetic, key_terms(): jnp.stack([key_grad.reshape(row_count, -1), value_grad.reshape(row_count,...  17.5 us
    dot_general x2, matrix products, key_terms(): jnp.einsum('chrk,crhs->khs', softmax_b, grad_rows, preferred_element_type...  15.4 us
    unnamed x33, local copies, waits for them, and re-layouts  10.6 us
    all_to_all x1, blocking collectives, local(): lax.all_to_all(self_keys[0], 'head', split_axis=1, concat_axis=0, tiled=T...  10 us
  transfers between devices with their start and end apart: 11, of which 7 were waited for; matrix products, arithmetic and copies ran while one was open for 31% of the time, Pallas kernels for 0%

commit v1 on v0

--- a/solution.py
+++ b/solution.py
@@ -4,6 +4,10 @@
 from jax.sharding import PartitionSpec as P
 
 MASK_FILL = -1e30
+
+
+def _view_vectors(v0):
+    return jax.lax.psum(jax.lax.psum(v0, axis_name="dp"), axis_name="seq")
 
 
 def page_layout(counts, widths, patch_total):
@@ -157,7 +161,7 @@
             self_dv.astype(jnp.bfloat16), "head", split_axis=0, concat_axis=1, tiled=True
         ),
     )
-    slope_grad = lax.psum(slope_local, ("seq", "dp")) / patch_total
+    slope_grad = _view_vectors(slope_local) / patch_total
     memory_all_keys, memory_all_values = (
         lax.all_gather(memory_keys[0], "seq", axis=0, tiled=True),
         lax.all_gather(memory_values[0], "seq", axis=0, tiled=True),

time: 408 us -> 362 us (0.89)
  blocking collectives: 149 us -> 53.9 us
  waiting for transfers between devices: 83.5 us -> 132 us
    psum x1 -> x2, blocking collectives: 129 us -> 34.6 us  [_view_vectors(): return jax.lax.psum(jax.lax.psum(v0, axis_name='dp'), axis_name='seq')]
    reduce_scatter x1, waiting for transfers between devices: 0.01 us -> 50.7 us  [local(): lax.psum_scatter(key_terms(text_ds_b, text_p_b, text_query_blocks, text_g...]
  transfers between devices with their start and end apart: 11 -> 11, of which waited for: 7 -> 7; matrix products, arithmetic and copies ran while one was open for 31% -> 35% of each run, Pallas kernels for 0% -> 0%
where the time goes in v1:
time: 362 us; the launch traced here: 360 us
  waiting for transfers between devices  132 us (36%)
  blocking collectives  53.9 us (15%)
  local copies, waits for them, and re-layouts  52.2 us (14%)
  matrix products  50.7 us (14%)
  other arithmetic  32.3 us (9%)
  starting transfers between devices  24.3 us (7%)
  between operations  14.4 us (4%)
    reduce_scatter x1, waiting for transfers between devices, local(): lax.psum_scatter(key_terms(text_ds_b, text_p_b, text_query_blocks, text_g...  50.7 us
    all_gather x1, waiting for transfers between devices, local(): lax.all_gather(local_values, 'seq', axis=0, tiled=True)  37.8 us
    psum x2, blocking collectives, _view_vectors(): return jax.lax.psum(jax.lax.psum(v0, axis_name='dp'), axis_name='seq')  34.6 us
    all_gather x1, waiting for transfers between devices, local(): lax.all_gather(memory_values[0], 'seq', axis=0, tiled=True)  27.1 us
    another operation x4, local copies, waits for them, and re-layouts, key_terms(): jnp.stack([key_grad.reshape(row_count, -1), value_grad.reshape(row_count,...  23.7 us
    another operation x2, other arithmetic, key_terms(): jnp.stack([key_grad.reshape(row_count, -1), value_grad.reshape(row_count,...  17.5 us
    dot_general x2, matrix products, key_terms(): jnp.einsum('chrk,crhs->khs', softmax_b, grad_rows, preferred_element_type...  15.4 us
    unnamed x33, local copies, waits for them, and re-layouts  10.6 us
  transfers between devices with their start and end apart: 11, of which 7 were waited for; matrix products, arithmetic and copies ran while one was open for 35% of the time, Pallas kernels for 0%

profile of v1, /device:TPU:2, one launch (start us, length us, event | category | flops | bytes accessed | tf_op | source)
XLA Modules:
  0.0 359.8 jit_solution(4920166462424637193)
XLA Ops:
  7.3 1.0 all_to_all.85
  8.3 10.0 %all_to_all.109 = bf16[32,4,640]{2,0,1:T(8,128)(2,1)} all-to-all(bf16[32,4,640]{2,0,1:T(8,128)(2,1)S(1)} %copy.117), channel_id=1, replica_groups=mesh['seq'=16,'head'=4,'dp'=4] {'head'}, dimensions={1} | all-to-all | bytes 327680 | tf_op jit(solution)/shard_map/all_to_all | solution.py:101
  18.4 1.0 all_to_all.92
  19.4 9.2 %all_to_all.110 = bf16[32,4,640]{2,0,1:T(8,128)(2,1)} all-to-all(bf16[32,4,640]{2,0,1:T(8,128)(2,1)S(1)} %copy.122), channel_id=1, replica_groups=mesh['seq'=16,'head'=4,'dp'=4] {'head'}, dimensions={1} | all-to-all | bytes 327680 | tf_op jit(solution)/shard_map/all_to_all | solution.py:102
  28.6 1.7 copy.136
  30.4 1.0 all_to_all.82
  31.4 0.7 copy.116
  32.1 4.7 %all-to-all-start = ((bf16[32,4,640]{2,0,1:T(8,128)(2,1)}), bf16[32,4,640]{2,0,1:T(8,128)(2,1)S(1)}, u32[]{:S(2)}, u32[]{:S(2)}) async-start(bf16[32,4,640]{2,0,1:T(8,128)(2,1)} %copy.116), calls=%async_computation | async-start | bytes 327680 | tf_op jit(solution)/shard_map/all_to_all | solution.py:100
  36.8 1.7 copy.140
  38.6 0.8 reduce-window.4
  39.4 0.7 fusion.25
  40.2 0.8 select_reduce_fusion.1
  41.4 1.8 abs_convert_fusion
  43.5 0.7 copy.121
  44.2 4.8 %all-to-all-start.2 = ((bf16[32,4,640]{2,0,1:T(8,128)(2,1)}), bf16[32,4,640]{2,0,1:T(8,128)(2,1)S(1)}, u32[]{:S(2)}, u32[]{:S(2)}) async-start(bf16[32,4,640]{2,0,1:T(8,128)(2,1)} %copy.121), calls=%async_computation.2 | async-start | bytes 327680 | tf_op jit(solution)/shard_map/all_to_all | solution.py:103
  49.4 4.3 %all-to-all-done.2 = bf16[32,4,640]{2,0,1:T(8,128)(2,1)S(1)} async-done(((bf16[32,4,640]{2,0,1:T(8,128)(2,1)}), bf16[32,4,640]{2,0,1:T(8,128)(2,1)S(1)}, u32[]{:S(2)}, u32[]{:S(2)}) %all-to-all-start.2) | async-done | bytes 163872 | tf_op jit(solution)/shard_map/all_to_all | solution.py:103
  54.1 6.2 %all-gather.7.cloned.1.call-done = bf16[2048,640]{1,0:T(8,128)(2,1)} async-done(((bf16[128,640]{1,0:T(8,128)(2,1)}), bf16[2048,640]{1,0:T(8,128)(2,1)}) %all-gather.7.cloned.1.call-update) | async-done | bytes 2621456 | tf_op jit(solution)/shard_map/all_gather | solution.py:108
  60.3 3.0 copy.118
  63.3 37.8 %all-gather.9.cloned.1.call-done = bf16[2048,640]{1,0:T(8,128)(2,1)} async-done(((bf16[128,640]{1,0:T(8,128)(2,1)}), bf16[2048,640]{1,0:T(8,128)(2,1)}) %all-gather.9.cloned.1.call-update) | async-done | bytes 2621456 | tf_op jit(solution)/shard_map/all_gather | solution.py:109
  101.0 4.5 %copy.123 = bf16[2048,640]{0,1:T(8,128)(2,1)} copy(bf16[2048,640]{1,0:T(8,128)(2,1)} %all-gather.9.cloned.1.call-done) | data formatting | bytes 5242880 | tf_op jit(solution)/shard_map/all_gather | solution.py:109
  105.5 3.6 select_add_fusion
  109.2 1.6 fusion.28
  110.8 1.0 copy-done.4
  111.8 1.0 copy-done.7
  112.8 1.3 multiply_reduce_fusion.3
  114.3 2.4 multiply_reduce_fusion.2
  116.7 3.2 convolution_multiply_fusion
  119.9 6.0 %copy.131 = f32[2048,1,640]{2,0,1:T(8,128)} copy(f32[2048,1,640]{0,2,1:T(8,128)} %bitcast.79) | data formatting | bytes 10485760 | tf_op jit(solution)/shard_map/stack;reshape | solution.py:81
  125.9 8.0 %fusion.7 = f32[5,2048,128]{1,2,0:T(8,128)} fusion(bf16[128,5,128]{0,2,1:T(8,128)(2,1)S(1)} %copy.130, f32[5,128]{1,0:T(8,128)S(1)} %get-tuple-element.85, f32[5,128,2048]{2,1,0:T(8,128)} %copy-done.4), kind=kOutput, calls=%fused_computation.22 | convolution fusion | flops 339479168 | bytes 10652160 | tf_op jit(solution)/shard_map/chrk,crhs->khs/dot_general | solution.py:78
  133.8 5.9 %copy.132 = f32[2048,1,640]{2,0,1:T(8,128)} copy(f32[2048,1,640]{0,2,1:T(8,128)} %bitcast.84) | data formatting | bytes 10485760 | tf_op jit(solution)/shard_map/stack;reshape | solution.py:81
  139.7 8.8 %pad_maximum_fusion = f32[2048,2,640]{2,0,1:T(8,128)} fusion(f32[2048,1,640]{2,0,1:T(8,128)} %copy.132, f32[2048,1,640]{2,0,1:T(8,128)} %copy.131), kind=kLoop, calls=%fused_computation.2 | loop fusion | flops 2621440 | bytes 20971520 | tf_op jit(solution)/shard_map/stack | solution.py:81
  148.8 0.7 copy-done.8
  149.7 1.1 copy.139
  150.8 1.6 compare_select_fusion
  152.4 9.5 %fusion.29 = (f32[5,256]{1,0:T(8,128)S(1)}, f32[5,256,2048]{2,1,0:T(8,128)}) fusion(f32[256,2048]{1,0:T(8,128)} %compare_select_fusion, bf16[256,5,128]{0,2,1:T(8,128)(2,1)S(1)} %bitcast.87, bf16[2048,5,128]{0,2,1:T(8,128)(2,1)} %bitcast.104), kind=kOutput, calls=%fused_computation.62 | convolution fusion | flops 681576448 | bytes 15537152 | tf_op jit(solution)/shard_map/while/body/eval_jaxpr/sub | solution.py:48
  161.9 27.1 %all-gather.13.cloned.1.call-done = bf16[1,2048,640]{1,2,0:T(8,128)(2,1)} async-done(((bf16[1,128,640]{1,2,0:T(8,128)(2,1)}), bf16[1,2048,640]{1,2,0:T(8,128)(2,1)}) %all-gather.13.cloned.1.call-update) | async-done | bytes 2621456 | tf_op jit(solution)/shard_map/all_gather | solution.py:167
  189.0 6.1 %multiply_reduce_fusion = (f32[5,256]{1,0:T(8,128)S(1)}, f32[5,256,2048]{2,1,0:T(8,128)S(1)}) fusion(f32[5,256,2048]{2,1,0:T(8,128)} %get-tuple-element.90, f32[5,256]{1,0:T(8,128)S(1)} %get-tuple-element.89, bf16[256,5,128]{0,2,1:T(8,128)(2,1)S(1)} %bitcast.96, bf16[2048,5,128]{0,2,1:T(8,128)(2,1)} %bitcast.106), kind=kOutput, calls=%fused_computation.5 | convolution fusion | flops 678951680 | bytes 23930880 | tf_op jit(solution)/shard_map/while/body/eval_jaxpr/rhs,khs->hrk/dot_general | solution.py:52
  195.1 1.1 slice-done.1
  196.2 0.6 slice-done.2
  196.8 1.8 multiply_convert_fusion
  198.6 3.9 %convolution_multiply_fusion.1 = f32[5,2048,128]{1,2,0:T(8,128)} fusion(bf16[256,5,128]{0,2,1:T(8,128)(2,1)S(1)} %bitcast.88, bf16[5,256,2048]{2,1,0:T(8,128)(2,1)S(1)} %multiply_convert_fusion), kind=kOutput, calls=%fused_computation.21 | convolution fusion | flops 672399360 | bytes 10813440 | tf_op jit(solution)/shard_map/chrk,crhs->khs/dot_general | solution.py:75
  202.6 5.9 %copy.143 = f32[2048,1,640]{2,0,1:T(8,128)} copy(f32[2048,1,640]{0,2,1:T(8,128)} %bitcast.78) | data formatting | bytes 10485760 | tf_op jit(solution)/shard_map/stack;reshape | solution.py:81
  208.5 7.4 %fusion.3 = f32[5,2048,128]{1,2,0:T(8,128)} fusion(bf16[256,5,128]{0,2,1:T(8,128)(2,1)S(1)} %bitcast.97, f32[5,256,2048]{2,1,0:T(8,128)} %get-tuple-element.90, f32[5,256]{1,0:T(8,128)S(1)} %get-tuple-element.89), kind=kOutput, calls=%fused_computation.9 | convolution fusion | flops 676331520 | bytes 16061440 | tf_op jit(solution)/shard_map/chrk,crhs->khs/dot_general | solution.py:78
  215.9 5.9 %copy.144 = f32[2048,1,640]{2,0,1:T(8,128)} copy(f32[2048,1,640]{0,2,1:T(8,128)} %bitcast.85) | data formatting | bytes 10485760 | tf_op jit(solution)/shard_map/stack;reshape | solution.py:81
  221.9 8.7 %pad_maximum_fusion.1 = f32[2048,2,640]{2,0,1:T(8,128)} fusion(f32[2048,1,640]{2,0,1:T(8,128)} %copy.144, f32[2048,1,640]{2,0,1:T(8,128)} %copy.143), kind=kLoop, calls=%fused_computation.3 | loop fusion | flops 2621440 | bytes 20971520 | tf_op jit(solution)/shard_map/stack | solution.py:81
  230.6 5.3 %fusion.14 = bf16[5,256,128]{1,2,0:T(8,128)(2,1)S(1)} fusion(bf16[5,256,2048]{2,1,0:T(8,128)(2,1)} %copy-done.2, bf16[2048,5,128]{0,2,1:T(8,128)(2,1)} %bitcast.105), kind=kOutput, calls=%fused_computation.31 | convolution fusion | flops 671416320 | bytes 8192000 | tf_op jit(solution)/shard_map/while/body/eval_jaxpr/hrk,khs->rhs/dot_general | solution.py:59
  235.9 10.5 %psum.14 = f32[2,5]{1,0:T(2,128)S(1)} all-reduce(f32[2,5]{1,0:T(2,128)S(1)} %maximum_negate_fusion), channel_id=1, replica_groups=mesh['seq'=16,'head'=4,'dp'=4] {'dp'}, use_global_device_ids=true, to_apply=%region_10.11 | all-reduce | flops 10 | bytes 80 | tf_op jit(solution)/shard_map/psum | solution.py:10
  246.4 0.9 copy.145
  247.3 24.2 %psum.15 = f32[2,5]{1,0:T(2,128)S(1)} all-reduce(f32[2,5]{1,0:T(2,128)S(1)} %psum.14), channel_id=1, replica_groups=mesh['seq'=16,'head'=4,'dp'=4] {'seq'}, use_global_device_ids=true, to_apply=%region_11.12 | all-reduce | flops 10 | bytes 80 | tf_op jit(solution)/shard_map/psum | solution.py:10
  271.5 2.6 fusion.21
  274.2 0.9 convert_element_type.95
  275.1 4.8 %all-to-all-start.4 = ((bf16[4,32,640]{2,1,0:T(8,128)(2,1)}), bf16[4,32,640]{2,1,0:T(8,128)(2,1)S(1)}, u32[]{:S(2)}, u32[]{:S(2)}) async-start(bf16[4,32,640]{2,1,0:T(8,128)(2,1)} %convert_element_type.95), calls=%async_computation.4 | async-start | bytes 327680 | tf_op jit(solution)/shard_map/all_to_all | solution.py:150
  279.9 1.1 convert.8
  281.0 0.8 fusion.27
  281.8 2.8 all-to-all-done.4
  284.6 4.8 %all-to-all-start.5 = ((bf16[4,32,640]{2,1,0:T(8,128)(2,1)}), bf16[4,32,640]{2,1,0:T(8,128)(2,1)S(1)}, u32[]{:S(2)}, u32[]{:S(2)}) async-start(bf16[4,32,640]{2,1,0:T(8,128)(2,1)} %bitcast.21), calls=%async_computation.6 | async-start | bytes 327680 | tf_op jit(solution)/shard_map/all_to_all | solution.py:157
  290.0 0.7 broadcast_in_dim.107
  290.8 50.7 %reduce-scatter.5.cloned.1.call-done = f32[128,2,640]{2,0,1:T(8,128)} async-done(((f32[2048,2,640]{2,0,1:T(8,128)}), f32[128,2,640]{2,0,1:T(8,128)}) %reduce-scatter.5.cloned.1.call-update) | async-done | bytes 655376 | tf_op jit(solution)/shard_map/reduce_scatter | solution.py:197
  341.4 1.1 convert.9
  342.6 4.8 %all-to-all-start.6 = ((bf16[4,32,640]{2,1,0:T(8,128)(2,1)}), bf16[4,32,640]{2,1,0:T(8,128)(2,1)S(1)}, u32[]{:S(2)}, u32[]{:S(2)}) async-start(bf16[4,32,640]{2,1,0:T(8,128)(2,1)} %bitcast.23), calls=%async_computation.7 | async-start | bytes 327680 | tf_op jit(solution)/shard_map/all_to_all | solution.py:160
  347.4 0.7 slice_bitcast_fusion
  348.2 0.7 broadcast_in_dim.108
  349.0 3.1 all-to-all-done.6
  352.2 0.7 broadcast_in_dim.109
  (62 shorter events, 3.7 us)
Async XLA Ops:
  7.2 143.6 %copy-start = (s32[1,4096]{1,0:T(1,128)S(1)}, s32[1,4096]{1,0:T(1,128)}, u32[]{:S(2)}) copy-start(s32[1,4096]{1,0:T(1,128)} %param.23) | copy-start | bytes 49156
  7.2 36.2 %copy-start.9 = (bf16[1,32,2560]{2,1,0:T(8,128)(2,1)S(1)}, bf16[1,32,2560]{2,1,0:T(8,128)(2,1)}, u32[]{:S(2)}) copy-start(bf16[1,32,2560]{2,1,0:T(8,128)(2,1)} %param.15) | copy-start | bytes 491524
  7.2 41.8 %copy-start.10 = (f32[2,5]{1,0:T(2,128)S(1)}, f32[2,5]{1,0:T(2,128)}, u32[]{:S(2)}) copy-start(f32[2,5]{1,0:T(2,128)} %param.20) | copy-start | bytes 124
  7.2 53.1 %all-gather.7.cloned.1.call-start = ((), (), s32[]{:S(2)}) async-start(), calls=%async_computation.9 | async-start | bytes 2785280 | tf_op jit(solution)/shard_map/all_gather | solution.py:108
  18.3 82.7 %all-gather.9.cloned.1.call-start = ((), (), s32[]{:S(2)}) async-start(), calls=%async_computation.10 | async-start | bytes 2785280 | tf_op jit(solution)/shard_map/all_gather | solution.py:109
  28.6 123.8 %all-gather.11.cloned.1.call-start = ((), (), s32[]{:S(2)}) async-start(), calls=%async_computation.13 | async-start | bytes 2785280 | tf_op jit(solution)/shard_map/all_gather | solution.py:166
  32.1 12.1 %all-to-all-start = ((bf16[32,4,640]{2,0,1:T(8,128)(2,1)}), bf16[32,4,640]{2,0,1:T(8,128)(2,1)S(1)}, u32[]{:S(2)}, u32[]{:S(2)}) async-start(bf16[32,4,640]{2,0,1:T(8,128)(2,1)} %copy.116), calls=%async_computation | async-start | bytes 327680 | tf_op jit(solution)/shard_map/all_to_all | solution.py:100
  36.8 152.1 %all-gather.13.cloned.1.call-start = ((), (), s32[]{:S(2)}) async-start(), calls=%async_computation.14 | async-start | bytes 2785280 | tf_op jit(solution)/shard_map/all_gather | solution.py:167
  44.2 9.5 %all-to-all-start.2 = ((bf16[32,4,640]{2,0,1:T(8,128)(2,1)}), bf16[32,4,640]{2,0,1:T(8,128)(2,1)S(1)}, u32[]{:S(2)}, u32[]{:S(2)}) async-start(bf16[32,4,640]{2,0,1:T(8,128)(2,1)} %copy.121), calls=%async_computation.2 | async-start | bytes 327680 | tf_op jit(solution)/shard_map/all_to_all | solution.py:103
  49.0 230.9 %reduce-scatter.3.cloned.1.call-start = ((), (), s32[]{:S(2)}) async-start(), calls=%async_computation.11 | async-start | bytes 11141120 | tf_op jit(solution)/shard_map/reduce_scatter | solution.py:135
  63.3 45.9 %copy-start.3 = (bf16[2048,640]{0,1:T(8,128)(2,1)}, bf16[2048,640]{0,1:T(8,128)(2,1)S(1)}, u32[]{:S(2)}) copy-start(bf16[2048,640]{0,1:T(8,128)(2,1)S(1)} %copy.118) | copy-start | bytes 7864324
  109.1 2.7 copy-start.4
  109.1 3.6 %copy-start.7 = (bf16[2048,640]{0,1:T(8,128)(2,1)S(1)}, bf16[2048,640]{0,1:T(8,128)(2,1)}, u32[]{:S(2)}) copy-start(bf16[2048,640]{0,1:T(8,128)(2,1)} %copy.123) | copy-start | bytes 7864324
  112.8 1.3 copy-start.5
  112.8 1.6 copy-start.6
  148.5 1.0 copy-start.8
  148.5 192.9 %reduce-scatter.5.cloned.1.call-start = ((), (), s32[]{:S(2)}) async-start(), calls=%async_computation.12 | async-start | bytes 11141120 | tf_op jit(solution)/shard_map/reduce_scatter | solution.py:197
  189.0 6.1 %slice-start = ((s8[10485760]{0:T(1024)(128)(4,1)}), s8[4194304]{0:T(1024)(128)(4,1)S(1)}, s32[]{:S(2)}) async-start(s8[10485760]{0:T(1024)(128)(4,1)} %bitcast.80), calls=%async_computation.15 | async-start | bytes 8388608
  189.0 7.3 %slice-start.1 = ((s8[10485760]{0:T(1024)(128)(4,1)}), s8[4194304]{0:T(1024)(128)(4,1)S(1)}, s32[]{:S(2)}) async-start(s8[10485760]{0:T(1024)(128)(4,1)} %bitcast.80), calls=%async_computation.16 | async-start | bytes 8388608
  189.0 7.9 %slice-start.2 = ((s8[10485760]{0:T(1024)(128)(4,1)}), s8[2097152]{0:T(1024)(128)(4,1)S(1)}, s32[]{:S(2)}) async-start(s8[10485760]{0:T(1024)(128)(4,1)} %bitcast.80), calls=%async_computation.17 | async-start | bytes 4194304
  198.6 4.0 %copy-start.2 = (bf16[5,256,2048]{2,1,0:T(8,128)(2,1)}, bf16[5,256,2048]{2,1,0:T(8,128)(2,1)S(1)}, u32[]{:S(2)}) copy-start(bf16[5,256,2048]{2,1,0:T(8,128)(2,1)S(1)} %multiply_convert_fusion) | copy-start | bytes 15728644
  247.3 105.6 %copy-start.1 = (s32[1,4096]{1,0:T(1,128)S(1)}, s32[1,4096]{1,0:T(1,128)}, u32[]{:S(2)}) copy-start(s32[1,4096]{1,0:T(1,128)} %param.23) | copy-start | bytes 49156
  275.1 9.5 %all-to-all-start.4 = ((bf16[4,32,640]{2,1,0:T(8,128)(2,1)}), bf16[4,32,640]{2,1,0:T(8,128)(2,1)S(1)}, u32[]{:S(2)}, u32[]{:S(2)}) async-start(bf16[4,32,640]{2,1,0:T(8,128)(2,1)} %convert_element_type.95), calls=%async_computation.4 | async-start | bytes 327680 | tf_op jit(solution)/shard_map/all_to_all | solution.py:150
  284.6 58.0 %all-to-all-start.5 = ((bf16[4,32,640]{2,1,0:T(8,128)(2,1)}), bf16[4,32,640]{2,1,0:T(8,128)(2,1)S(1)}, u32[]{:S(2)}, u32[]{:S(2)}) async-start(bf16[4,32,640]{2,1,0:T(8,128)(2,1)} %bitcast.21), calls=%async_computation.6 | async-start | bytes 327680 | tf_op jit(solution)/shard_map/all_to_all | solution.py:157
  342.6 9.5 %all-to-all-start.6 = ((bf16[4,32,640]{2,1,0:T(8,128)(2,1)}), bf16[4,32,640]{2,1,0:T(8,128)(2,1)S(1)}, u32[]{:S(2)}, u32[]{:S(2)}) async-start(bf16[4,32,640]{2,1,0:T(8,128)(2,1)} %bitcast.23), calls=%async_computation.7 | async-start | bytes 327680 | tf_op jit(solution)/shard_map/all_to_all | solution.py:160
Sparse Core Ops, SparseCore 0:
  18.4 41.7 all-gather.6
  62.1 38.8 all-gather.8
  103.4 41.4 all-gather.10
  147.0 41.9 all-gather.12
  191.4 73.5 reduce-scatter.2
  267.4 74.0 reduce-scatter.4
